TPU v7x, 256 devices: a whole 4x4x8 slice. The times are simulated.
256 devices in a mesh: harm: 8 (over z_lo, core), prop: 32 (over z_hi, y, x).
Axes of the slice: x: 4, y: 4, z: 8 (z_hi: 2, z_lo: 4; z = z_hi * 4 + z_lo), core: 2. Of those that a mesh axis runs over, the one named last changes fastest.
Arguments:
- rhs_field: float32 [2, 6, 64, 65536], P(None, None, 'harm', 'prop'), may hold values from -48 to 48
- field_guess: float32 [2, 6, 64, 65536], P(None, None, 'harm', 'prop'), may hold values from -6 to 6
- permittivity: float32 [65536], P('prop'), may hold values from 1 to 4
- mod_cells: int32 [32, 640], P('prop'), may hold values from 0 to 2047, as said below
- mod_count: int32 [32], P('prop'), may hold values from 80 to 640
- mod_profile: int32 [32, 640], P('prop'), may hold values from 0 to 15
- mod_amp: float32 [16], replicated, may hold values from 0.25 to 1
- mod_phase: float32 [16], replicated, may hold values from -3.140625 to 3.140625
Outputs:
- fields: float32 [2, 6, 64, 65536], P(None, None, 'harm', 'prop')
Inputs may be any that keep to these rules, and one draw needn't show every extreme that they name: `mod_cells`: each slab's list names 640 different cells of that slab.
All inputs are finite; a program needn't handle non-finite values.
Results may differ from a plain program's by a relative error of at most 0.0003.
Values sent between devices are 32-bit elements; how exact they have to be, the bound alone decides.
A program may use at most 256 MiB of HBM per device.

v0:
```python
import functools

import jax
import jax.numpy as jnp
from jax import lax
from jax.experimental import pallas as pl
from jax.experimental.pallas import tpu as pltpu
from jax.sharding import PartitionSpec as P

HARMONICS = 64
TX = 64
BASE_FREQUENCY = 6.0
MOD_FREQUENCY = 0.05
WAVE_NUMBER = 0.3
PROFILES = 16
MESH = pl.DeviceIdType.MESH
LANES = 128
BLOCK = 512
CHUNKS = 8


def remote(src, dst, send, recv, device):
    return pltpu.make_async_remote_copy(
        src_ref=src, dst_ref=dst, send_sem=send, recv_sem=recv, device_id=device, device_id_type=MESH
    )


def signal(condition, sem, device):
    @pl.when(condition)
    def _():
        pl.semaphore_signal(sem, inc=1, device_id=device, device_id_type=MESH)


def mod_tables(plane, cells, profile, count, amp, phase):
    row = lax.broadcasted_iota(jnp.int32, (PROFILES, LANES), 0)
    amps = jnp.zeros((PROFILES, LANES), jnp.float32)
    phases = jnp.zeros((PROFILES, LANES), jnp.float32)
    for i in range(PROFILES):
        amps = jnp.where(row == i, amp[i], amps)
        phases = jnp.where(row == i, phase[i], phases)
    angle = phases - WAVE_NUMBER * plane
    cosines = 0.5 * amps * jnp.cos(angle)
    sines = 0.5 * amps * jnp.sin(angle)
    length = cells.shape[1]
    live = count[0]
    lane = lax.broadcasted_iota(jnp.int32, (1, LANES), 1)
    low_row = lax.broadcasted_iota(jnp.int32, (LANES, LANES), 0)
    left, right = [], []
    for j in range(length // LANES):
        part = slice(j * LANES, (j + 1) * LANES)
        cell, prof = cells[:, part], profile[:, part]
        active = (lane + j * LANES) < live
        here = (row == cell // LANES) & active
        hit = row == prof
        cosine = jnp.sum(jnp.where(hit, cosines, 0.0), axis=0, keepdims=True)
        sine = jnp.sum(jnp.where(hit, sines, 0.0), axis=0, keepdims=True)
        left.append(
            jnp.concatenate([jnp.where(here, cosine, 0.0), jnp.where(here, sine, 0.0)], axis=0)
        )
        right.append((low_row == cell % LANES).astype(jnp.float32))
    return lax.dot_general(
        jnp.concatenate(left, axis=1),
        jnp.concatenate(right, axis=1),
        (((1,), (1,)), ((), ())),
        precision=lax.Precision.HIGHEST,
        preferred_element_type=jnp.float32,
    )


def partial_sweep(fields, rhs, low_edge, high_edge, tab, a, out, cells):
    width = min(BLOCK, cells)
    wide = width + LANES
    lane = lax.broadcasted_iota(jnp.int32, (8, width), 1)
    column = lane % TX
    not_last, not_first = column != TX - 1, column != 0
    row = lax.broadcasted_iota(jnp.int32, (8, width), 0)

    def body(step, carry):
        at = pl.multiple_of(step * width, LANES)
        here = pl.ds(at, width)
        mid = pl.ds(pl.multiple_of(at + LANES, LANES), width)

        def ahead(c, k):
            v = fields[c, k, :, pl.ds(pl.multiple_of(at + LANES, LANES), wide)]
            own = v[:, :width]
            dy = pltpu.roll(v, wide - TX, 1)[:, :width] - own
            dx = jnp.where(not_last, pltpu.roll(v, wide - 1, 1)[:, :width], 0.0) - own
            return own, dy, dx

        def behind(c, k):
            v = fields[c, k, :, pl.ds(at, wide)]
            own = v[:, LANES:]
            dy = own - pltpu.roll(v, TX, 1)[:, LANES:]
            dx = own - jnp.where(not_first, pltpu.roll(v, 1, 1)[:, LANES:], 0.0)
            return own, dy, dx

        cos_t, sin_t, ae = (tab[i, :, here] for i in range(3))
        couple = []
        for k in range(3):
            low, high = [], []
            for c in range(2):
                v = fields[c, k, :, mid]
                i = c * 3 + k
                low.append(jnp.where(row == 0, low_edge[i : i + 1, here], pltpu.roll(v, 1, 0)))
                high.append(jnp.where(row == 7, high_edge[i : i + 1, here], pltpu.roll(v, 7, 0)))
            couple.append(
                (
                    cos_t * (low[0] + high[0]) + sin_t * (high[1] - low[1]),
                    cos_t * (low[1] + high[1]) + sin_t * (low[0] - high[0]),
                )
            )
        for c in range(2):
            s = 1.0 if c == 1 else -1.0
            ex, ex_y, _ = ahead(c, 0)
            ey, _, ey_x = ahead(c, 1)
            _, ez_y, ez_x = ahead(c, 2)
            sa = s * a
            out(3, 1 - c, here, sa * (rhs[c, 3, :, here] - ez_y - ey))
            out(4, 1 - c, here, sa * (rhs[c, 4, :, here] + ex + ez_x))
            out(5, 1 - c, here, sa * (rhs[c, 5, :, here] - ey_x + ex_y))
            hx, hx_y, _ = behind(c, 3)
            hy, _, hy_x = behind(c, 4)
            _, hz_y, hz_x = behind(c, 5)
            sae = s * ae
            out(0, 1 - c, here, sae * (rhs[c, 0, :, here] + hz_y - hy) - couple[0][1 - c])
            out(1, 1 - c, here, sae * (rhs[c, 1, :, here] + hx - hz_x) - couple[1][1 - c])
            out(2, 1 - c, here, sae * (rhs[c, 2, :, here] + hy_x - hx_y) - couple[2][1 - c])
        return carry

    lax.fori_loop(0, cells // width, body, 0)


def kernel(
    rhs_hbm, field_hbm, eps_hbm, cells_hbm, profile_hbm, count, amp, phase, out_hbm,
    x, y, rhs, res, p_own, q_own, e_next, h_prev, p_next, q_prev, eps, eps_next, cells, profile,
    tab, low_out, high_out, low_in, high_in,
    local_sem, out_sem, eps_sem, edge_send, edge_recv, down_send, down_recv, up_send, up_recv,
):
    h, p = lax.axis_index("harm"), lax.axis_index("prop")
    nh, np_ = lax.axis_size("harm"), lax.axis_size("prop")
    size = rhs.shape[3]
    chunk = size // CHUNKS
    below, above = {"prop": p - 1}, {"prop": p + 1}
    has_below, has_above = p > 0, p < np_ - 1
    has_low, has_high = h > 0, h < nh - 1

    barrier = pltpu.get_barrier_semaphore()
    signal(has_below, barrier, below)
    signal(has_above, barrier, above)
    signal(has_low, barrier, {"harm": h - 1})
    signal(has_high, barrier, {"harm": h + 1})

    interior = slice(LANES, LANES + size)
    loads = [
        pltpu.make_async_copy(field_hbm, x.at[:, :, :, interior], local_sem.at[0]),
        pltpu.make_async_copy(rhs_hbm, rhs, local_sem.at[1]),
        pltpu.make_async_copy(eps_hbm, eps, local_sem.at[2]),
        pltpu.make_async_copy(cells_hbm, cells, local_sem.at[3]),
        pltpu.make_async_copy(profile_hbm, profile, local_sem.at[4]),
    ]
    for load in loads:
        load.start()

    neighbours = (
        has_below.astype(jnp.int32) + has_above.astype(jnp.int32)
        + has_low.astype(jnp.int32) + has_high.astype(jnp.int32)
    )
    pl.semaphore_wait(barrier, neighbours)

    def lanes(c):
        return slice(c * chunk, (c + 1) * chunk)

    def down(sweep, c):
        src = field_hbm.at[:, 0:2, :, lanes(c)] if sweep == 0 else p_own.at[:, :, :, lanes(c)]
        dst = (e_next, p_next)[sweep].at[:, :, :, lanes(c)]
        return remote(src, dst, down_send.at[sweep, c], down_recv.at[sweep, c], below)

    def up(sweep, c):
        src = field_hbm.at[:, 3:5, :, lanes(c)] if sweep == 0 else q_own.at[:, :, :, lanes(c)]
        dst = (h_prev, q_prev)[sweep].at[:, :, :, lanes(c)]
        return remote(src, dst, up_send.at[sweep, c], up_recv.at[sweep, c], above)

    eps_copy = remote(eps_hbm, eps_next, eps_sem.at[0], eps_sem.at[1], below)

    def start_sweep(sweep):
        for c in range(CHUNKS):

            @pl.when(has_below)
            def _():
                down(sweep, c).start()

            @pl.when(has_above)
            def _():
                up(sweep, c).start()

    start_sweep(0)

    @pl.when(has_below)
    def _():
        eps_copy.start()

    def to_low(sweep):
        return remote(
            low_out.at[sweep], high_in.at[sweep], edge_send.at[sweep, 0], edge_recv.at[sweep, 0],
            {"harm": h - 1},
        )

    def to_high(sweep):
        return remote(
            high_out.at[sweep], low_in.at[sweep], edge_send.at[sweep, 1], edge_recv.at[sweep, 1],
            {"harm": h + 1},
        )

    def send_edges(sweep, fields):
        for c in range(2):
            for k in range(3):
                i = c * 3 + k
                low_out[sweep, i : i + 1, :] = fields[c, k, 0:1, interior]
                high_out[sweep, i : i + 1, :] = fields[c, k, 7:8, interior]

        @pl.when(has_low)
        def _():
            to_low(sweep).start()

        @pl.when(has_high)
        def _():
            to_high(sweep).start()

    def wait_edges(sweep):
        @pl.when(has_high)
        def _():
            to_low(sweep).wait_recv()

        @pl.when(has_low)
        def _():
            to_high(sweep).wait_recv()

    for sweep in range(2):
        low_out[sweep, 6:8, :] = jnp.zeros((2, size), jnp.float32)
        high_out[sweep, 6:8, :] = jnp.zeros((2, size), jnp.float32)
    loads[0].wait()
    send_edges(0, x)

    @pl.when(jnp.logical_not(has_low))
    def _():
        low_in[...] = jnp.zeros_like(low_in)

    @pl.when(jnp.logical_not(has_high))
    def _():
        high_in[...] = jnp.zeros_like(high_in)

    @pl.when(jnp.logical_not(has_below))
    def _():
        h_prev[...] = jnp.zeros_like(h_prev)
        q_prev[...] = jnp.zeros_like(q_prev)

    @pl.when(jnp.logical_not(has_above))
    def _():
        e_next[...] = jnp.zeros_like(e_next)
        p_next[...] = jnp.zeros_like(p_next)
        eps_next[...] = jnp.ones_like(eps_next)

    pad = jnp.zeros((2, 3, 8, LANES), jnp.float32)
    for fields in (x, y):
        fields[:, 0:3, :, LANES + size :] = pad
        fields[:, 3:6, :, :LANES] = pad

    harmonic = h * 8 + lax.broadcasted_iota(jnp.int32, (8, 1), 0)
    omega = BASE_FREQUENCY + MOD_FREQUENCY * (harmonic - HARMONICS // 2).astype(jnp.float32)
    a = 1.0 / omega
    for load in loads[2:]:
        load.wait()
    dense = mod_tables(p.astype(jnp.float32), cells[...], profile[...], count, amp, phase)
    for i in range(size // LANES):
        part = slice(i * LANES, (i + 1) * LANES)
        inverse = 1.0 / eps[:, part]
        tab[0, :, part] = jnp.broadcast_to(dense[i : i + 1, :] * inverse, (8, LANES))
        tab[1, :, part] = jnp.broadcast_to(dense[PROFILES + i : PROFILES + i + 1, :] * inverse, (8, LANES))
        tab[2, :, part] = a * inverse
    loads[1].wait()
    wait_edges(0)

    def to_first(k, c, here, value):
        if k in (0, 1):
            p_own[c, k, :, here] = value
        elif k in (3, 4):
            q_own[c, k - 3, :, here] = value
        else:
            y[c, k, :, pl.ds(pl.multiple_of(here.start + LANES, LANES), here.size)] = value

    partial_sweep(x, rhs, low_in.at[0], high_in.at[0], tab, a, to_first, size)
    start_sweep(1)

    for c in range(CHUNKS):

        @pl.when(has_above)
        def _():
            down(0, c).wait_recv()

        @pl.when(has_below)
        def _():
            up(0, c).wait_recv()

        part = lanes(c)
        wide = slice(LANES + c * chunk, LANES + (c + 1) * chunk)
        ae = tab[2, :, part]
        for i in range(2):
            s = 1.0 if i == 1 else -1.0
            y[1 - i, 0, :, wide] = p_own[1 - i, 0, :, part] + s * ae * h_prev[i, 1, :, part]
            y[1 - i, 1, :, wide] = p_own[1 - i, 1, :, part] - s * ae * h_prev[i, 0, :, part]
            y[1 - i, 3, :, wide] = q_own[1 - i, 0, :, part] + s * a * e_next[i, 1, :, part]
            y[1 - i, 4, :, wide] = q_own[1 - i, 1, :, part] - s * a * e_next[i, 0, :, part]

    send_edges(1, y)

    @pl.when(has_above)
    def _():
        eps_copy.wait_recv()

    above_factor = has_above.astype(jnp.float32)
    below_factor = has_below.astype(jnp.float32)
    wait_edges(1)

    def to_second(k, c, here, value):
        res[c, k, :, here] = value

    partial_sweep(y, rhs, low_in.at[1], high_in.at[1], tab, a, to_second, size)
    outs = [
        pltpu.make_async_copy(res.at[:, k], out_hbm.at[:, k], out_sem.at[0, i])
        for i, k in enumerate((2, 5))
    ]
    for copy in outs:
        copy.start()

    for c in range(CHUNKS):
        part = lanes(c)
        wide = slice(LANES + c * chunk, LANES + (c + 1) * chunk)

        @pl.when(has_above)
        def _():
            down(1, c).wait_recv()

        @pl.when(has_below)
        def _():
            up(1, c).wait_recv()

        ae = tab[2, :, part]
        ae_next = a * (above_factor / eps_next[:, part])
        a_below = a * below_factor
        for i in range(2):
            s = 1.0 if i == 1 else -1.0
            j = 1 - i
            ex = p_next[i, 0, :, part] - s * ae_next * x[j, 4, :, wide]
            ey = p_next[i, 1, :, part] + s * ae_next * x[j, 3, :, wide]
            hx = q_prev[i, 0, :, part] - s * a_below * x[j, 1, :, wide]
            hy = q_prev[i, 1, :, part] + s * a_below * x[j, 0, :, wide]
            res[j, 0, :, part] += s * ae * hy
            res[j, 1, :, part] -= s * ae * hx
            res[j, 3, :, part] += s * a * ey
            res[j, 4, :, part] -= s * a * ex
        for i, k in enumerate((0, 3)):
            copy = pltpu.make_async_copy(
                res.at[:, k : k + 2, :, part], out_hbm.at[:, k : k + 2, :, part], out_sem.at[c + 1, i]
            )
            copy.start()
            outs.append(copy)

    @pl.when(has_below)
    def _():
        eps_copy.wait_send()

    for sweep in range(2):

        @pl.when(has_low)
        def _():
            to_low(sweep).wait_send()

        @pl.when(has_high)
        def _():
            to_high(sweep).wait_send()

        for c in range(CHUNKS):

            @pl.when(has_below)
            def _():
                down(sweep, c).wait_send()

            @pl.when(has_above)
            def _():
                up(sweep, c).wait_send()

    for copy in outs:
        copy.wait()


def local(rhs_field, field_guess, permittivity, mod_cells, mod_count, mod_profile, mod_amp, mod_phase):
    size = permittivity.shape[0]
    listed = mod_cells.shape[1]
    f32 = jnp.float32
    whole = (2, 6, 8, size)
    padded = (2, 6, 8, size + 2 * LANES)
    face = (2, 2, 8, size)
    dma = pltpu.SemaphoreType.DMA
    anywhere, smem = pl.BlockSpec(memory_space=pl.ANY), pl.BlockSpec(memory_space=pltpu.SMEM)
    return pl.pallas_call(
        kernel,
        out_shape=jax.ShapeDtypeStruct(whole, f32),
        in_specs=[anywhere] * 5 + [smem] * 3,
        out_specs=anywhere,
        scratch_shapes=[
            pltpu.VMEM(padded, f32), pltpu.VMEM(padded, f32), pltpu.VMEM(whole, f32), pltpu.VMEM(whole, f32),
            *[pltpu.VMEM(face, f32)] * 6,
            pltpu.VMEM((1, size), f32), pltpu.VMEM((1, size), f32),
            pltpu.VMEM((1, listed), jnp.int32), pltpu.VMEM((1, listed), jnp.int32),
            pltpu.VMEM((3, 8, size), f32),
            *[pltpu.VMEM((2, 8, size), f32)] * 4,
            dma((5,)), dma((CHUNKS + 1, 2)), dma((2,)), dma((2, 2)), dma((2, 2)),
            *[dma((2, CHUNKS))] * 4,
        ],
        compiler_params=pltpu.CompilerParams(
            collective_id=0, has_side_effects=True, vmem_limit_bytes=60 * 2**20
        ),
        name="sweeps",
    )(rhs_field, field_guess, permittivity.reshape(1, size), mod_cells, mod_profile, mod_count, mod_amp, mod_phase)


def solution(mesh):
    return jax.shard_map(
        local,
        mesh=mesh,
        in_specs=(
            P(None, None, "harm", "prop"),
            P(None, None, "harm", "prop"),
            P("prop"),
            P("prop", None),
            P("prop"),
            P("prop", None),
            P(),
            P(),
        ),
        out_specs=P(None, None, "harm", "prop"),
        check_vma=False,
    )
```

profile of v0, /device:TPU:31, one launch (start us, length us, event | category | flops | bytes accessed | tf_op | source)
XLA Modules:
  0.0 38.9 jit_solution(14109792782586603)
XLA Ops:
  0.7 36.2 %sweeps.1 = f32[2,6,8,2048]{3,2,1,0:T(8,128)} custom-call(f32[2,6,8,2048]{3,2,1,0:T(8,128)} %rhs_hbm.1, f32[2,6,8,2048]{3,2,1,0:T(8,128)} %field_hbm.1, f32[1,2048]{1,0:T(1,128)} %bitcast.1, s32[1,640]{1,0:T(1,128)} %cells_hbm.1, s32[1,640]{1,0:T(1,128)} %profile_hbm.1, s32[1]{0:T(128)S(6)} %copy.10.count, f32[16]{0:T(128)} %amp.1, f32[16]{0:T(128)} %phase.1), custom_call_target="tpu_custom_call" | custom-call | tf_op jit(solution)/shard_map/sweeps/pallas_call | solution.py:405
  36.9 2.1 %copy.11 = f32[2,6,8,2048]{3,2,1,0:T(8,128)} copy(f32[2,6,8,2048]{3,2,1,0:T(8,128)} %sweeps.1) | data formatting | bytes 1572864
where the time goes:
time: 39.5 us; the launch traced here: 38.9 us
  Pallas kernels  36.2 us (92%)
  local copies, waits for them, and re-layouts  2.06 us (5%)
  between operations  0.66 us (2%)
    pallas_call x1, Pallas kernels, local(): pl.pallas_call(kernel, out_shape=jax.ShapeDtypeStruct(whole, f32), in_spe...  36.2 us
    unnamed x1, local copies, waits for them, and re-layouts  2.06 us

commit v1 on v0

--- a/solution.py
+++ b/solution.py
@@ -17,6 +17,16 @@
 LANES = 128
 BLOCK = 512
 CHUNKS = 8
+LAST = 15
+UP_BY, DOWN_BY = (0, 3), (31, 28)
+WAYS = ((1, 2, 0, 1, 2, 0, 1, 0), (1, 2, 0, 2, 1, 0, 2, 0))
+SLOTS = 3
+RELAYED = [
+    (sweep, c, way, WAYS[sweep][:c].count(way))
+    for sweep in range(2)
+    for c, way in enumerate(WAYS[sweep])
+    if way
+]
 
 
 def remote(src, dst, send, recv, device):
@@ -134,7 +144,7 @@
     rhs_hbm, field_hbm, eps_hbm, cells_hbm, profile_hbm, count, amp, phase, out_hbm,
     x, y, rhs, res, p_own, q_own, e_next, h_prev, p_next, q_prev, eps, eps_next, cells, profile,
     tab, low_out, high_out, low_in, high_in,
-    local_sem, out_sem, eps_sem, edge_send, edge_recv, down_send, down_recv, up_send, up_recv,
+    passing, pass_recv, pass_send, local_sem, out_sem, eps_sem, edge_send, edge_recv, down_send, down_recv, up_send, up_recv,
 ):
     h, p = lax.axis_index("harm"), lax.axis_index("prop")
     nh, np_ = lax.axis_size("harm"), lax.axis_size("prop")
@@ -165,33 +175,72 @@
         has_below.astype(jnp.int32) + has_above.astype(jnp.int32)
         + has_low.astype(jnp.int32) + has_high.astype(jnp.int32)
     )
+    far = [(LAST, by, LAST + 1) for by in UP_BY] + [(LAST + 1, by, LAST) for by in DOWN_BY]
+    for start, by, end in far:
+        signal(p == by, barrier, {"prop": start})
+        signal(p == end, barrier, {"prop": by})
+        neighbours += (p == start).astype(jnp.int32) + (p == by).astype(jnp.int32)
     pl.semaphore_wait(barrier, neighbours)
 
     def lanes(c):
         return slice(c * chunk, (c + 1) * chunk)
 
-    def down(sweep, c):
+    def down_parts(sweep, c):
         src = field_hbm.at[:, 0:2, :, lanes(c)] if sweep == 0 else p_own.at[:, :, :, lanes(c)]
         dst = (e_next, p_next)[sweep].at[:, :, :, lanes(c)]
-        return remote(src, dst, down_send.at[sweep, c], down_recv.at[sweep, c], below)
-
-    def up(sweep, c):
+        return src, dst, down_send.at[sweep, c], down_recv.at[sweep, c]
+
+    def down(sweep, c):
+        return remote(*down_parts(sweep, c), below)
+
+    def up_parts(sweep, c):
         src = field_hbm.at[:, 3:5, :, lanes(c)] if sweep == 0 else q_own.at[:, :, :, lanes(c)]
         dst = (h_prev, q_prev)[sweep].at[:, :, :, lanes(c)]
-        return remote(src, dst, up_send.at[sweep, c], up_recv.at[sweep, c], above)
+        return src, dst, up_send.at[sweep, c], up_recv.at[sweep, c]
+
+    def up(sweep, c):
+        return remote(*up_parts(sweep, c), above)
 
     eps_copy = remote(eps_hbm, eps_next, eps_sem.at[0], eps_sem.at[1], below)
 
+    def to_pass(sweep, c, i, is_up, by):
+        src, _, send, _ = (up_parts if is_up else down_parts)(sweep, c)
+        return remote(src, passing.at[sweep, i], send, pass_recv.at[sweep, i], {"prop": by})
+
+    def pass_on(sweep, c, i, is_up):
+        _, dst, _, recv = (up_parts if is_up else down_parts)(sweep, c)
+        end = LAST + 1 if is_up else LAST
+        return remote(passing.at[sweep, i], dst, pass_send.at[sweep, i], recv, {"prop": end})
+
     def start_sweep(sweep):
+        for at, c, way, i in RELAYED:
+            if at == sweep:
+                for is_up, start, by in ((True, LAST, UP_BY[way - 1]), (False, LAST + 1, DOWN_BY[way - 1])):
+
+                    @pl.when(p == start)
+                    def _():
+                        to_pass(sweep, c, i, is_up, by).start()
+
         for c in range(CHUNKS):
-
-            @pl.when(has_below)
+            straight = WAYS[sweep][c] == 0
+
+            @pl.when(has_below if straight else has_below & (p != LAST + 1))
             def _():
                 down(sweep, c).start()
 
-            @pl.when(has_above)
+            @pl.when(has_above if straight else has_above & (p != LAST))
             def _():
                 up(sweep, c).start()
+
+    def pass_all(sweep):
+        for at, c, way, i in RELAYED:
+            if at == sweep:
+                for is_up, by in ((True, UP_BY[way - 1]), (False, DOWN_BY[way - 1])):
+
+                    @pl.when(p == by)
+                    def _():
+                        to_pass(sweep, c, i, is_up, by).wait_recv()
+                        pass_on(sweep, c, i, is_up).start()
 
     start_sweep(0)
 
@@ -312,6 +361,8 @@
             y[1 - i, 4, :, wide] = q_own[1 - i, 1, :, part] - s * a * e_next[i, 0, :, part]
 
     send_edges(1, y)
+    pass_all(0)
+    pass_all(1)
 
     @pl.when(has_above)
     def _():
@@ -388,6 +439,13 @@
             @pl.when(has_above)
             def _():
                 up(sweep, c).wait_send()
+
+    for sweep, c, way, i in RELAYED:
+        for is_up, by in ((True, UP_BY[way - 1]), (False, DOWN_BY[way - 1])):
+
+            @pl.when(p == by)
+            def _():
+                pass_on(sweep, c, i, is_up).wait_send()
 
     for copy in outs:
         copy.wait()
@@ -414,6 +472,7 @@
             pltpu.VMEM((1, listed), jnp.int32), pltpu.VMEM((1, listed), jnp.int32),
             pltpu.VMEM((3, 8, size), f32),
             *[pltpu.VMEM((2, 8, size), f32)] * 4,
+            pltpu.VMEM((2, SLOTS, 2, 2, 8, size // CHUNKS), f32), dma((2, SLOTS)), dma((2, SLOTS)),
             dma((5,)), dma((CHUNKS + 1, 2)), dma((2,)), dma((2, 2)), dma((2, 2)),
             *[dma((2, CHUNKS))] * 4,
         ],

time: 39.5 us -> 32.8 us (0.83); the launches traced: 38.9 us -> 32.7 us
  Pallas kernels: 36.2 us -> 29.9 us
    pallas_call x1, Pallas kernels: 36.2 us -> 29.9 us  [local(): pl.pallas_call(kernel, out_shape=jax.ShapeDtypeStruct(whole, f32), in_spe...]
where the time goes in v1:
time: 32.8 us; the launch traced here: 32.7 us
  Pallas kernels  29.9 us (91%)
  local copies, waits for them, and re-layouts  2.06 us (6%)
  between operations  0.66 us (2%)
    pallas_call x1, Pallas kernels, local(): pl.pallas_call(kernel, out_shape=jax.ShapeDtypeStruct(whole, f32), in_spe...  29.9 us
    unnamed x1, local copies, waits for them, and re-layouts  2.06 us

profile of v1, /device:TPU:31, one launch (start us, length us, event | category | flops | bytes accessed | tf_op | source)
XLA Modules:
  0.0 32.7 jit_solution(12867178989017978144)
XLA Ops:
  0.7 29.9 %sweeps.1 = f32[2,6,8,2048]{3,2,1,0:T(8,128)} custom-call(f32[2,6,8,2048]{3,2,1,0:T(8,128)} %rhs_hbm.1, f32[2,6,8,2048]{3,2,1,0:T(8,128)} %field_hbm.1, f32[1,2048]{1,0:T(1,128)} %bitcast.1, s32[1,640]{1,0:T(1,128)} %cells_hbm.1, s32[1,640]{1,0:T(1,128)} %profile_hbm.1, s32[1]{0:T(128)S(6)} %copy.10.count, f32[16]{0:T(128)} %amp.1, f32[16]{0:T(128)} %phase.1), custom_call_target="tpu_custom_call" | custom-call | tf_op jit(solution)/shard_map/sweeps/pallas_call | solution.py:463
  30.6 2.1 %copy.11 = f32[2,6,8,2048]{3,2,1,0:T(8,128)} copy(f32[2,6,8,2048]{3,2,1,0:T(8,128)} %sweeps.1) | data formatting | bytes 1572864

commit v2 on v1

--- a/solution.py
+++ b/solution.py
@@ -18,9 +18,9 @@
 BLOCK = 512
 CHUNKS = 8
 LAST = 15
-UP_BY, DOWN_BY = (0, 3), (31, 28)
-WAYS = ((1, 2, 0, 1, 2, 0, 1, 0), (1, 2, 0, 2, 1, 0, 2, 0))
-SLOTS = 3
+UP_BY, DOWN_BY = (0, 3, 12), (31, 28, 19)
+WAYS = ((1, 2, 3, 0, 1, 2, 3, 0), (1, 2, 3, 0, 1, 2, 0, 0))
+SLOTS = 2
 RELAYED = [
     (sweep, c, way, WAYS[sweep][:c].count(way))
     for sweep in range(2)
@@ -144,7 +144,7 @@
     rhs_hbm, field_hbm, eps_hbm, cells_hbm, profile_hbm, count, amp, phase, out_hbm,
     x, y, rhs, res, p_own, q_own, e_next, h_prev, p_next, q_prev, eps, eps_next, cells, profile,
     tab, low_out, high_out, low_in, high_in,
-    passing, pass_recv, pass_send, local_sem, out_sem, eps_sem, edge_send, edge_recv, down_send, down_recv, up_send, up_recv,
+    far_sem, passing, pass_recv, pass_send, local_sem, out_sem, eps_sem, edge_send, edge_recv, down_send, down_recv, up_send, up_recv,
 ):
     h, p = lax.axis_index("harm"), lax.axis_index("prop")
     nh, np_ = lax.axis_size("harm"), lax.axis_size("prop")
@@ -154,11 +154,23 @@
     has_below, has_above = p > 0, p < np_ - 1
     has_low, has_high = h > 0, h < nh - 1
 
+    near_above, near_below = has_above & (p != LAST), has_below & (p != LAST + 1)
+    sides = [(LAST, LAST + 1, UP_BY), (LAST + 1, LAST, DOWN_BY)]
     barrier = pltpu.get_barrier_semaphore()
-    signal(has_below, barrier, below)
-    signal(has_above, barrier, above)
+    signal(near_below, barrier, below)
+    signal(near_above, barrier, above)
     signal(has_low, barrier, {"harm": h - 1})
     signal(has_high, barrier, {"harm": h + 1})
+    neighbours = sum(
+        condition.astype(jnp.int32) for condition in (near_below, near_above, has_low, has_high)
+    )
+    for start, end, (first, *others) in sides:
+        greetings = [(first, start), (start, first), (end, first)]
+        for other in others:
+            greetings += [(other, start), (other, first)]
+        for source, target in greetings:
+            signal(p == source, barrier, {"prop": target})
+            neighbours += (p == target).astype(jnp.int32)
 
     interior = slice(LANES, LANES + size)
     loads = [
@@ -171,16 +183,10 @@
     for load in loads:
         load.start()
 
-    neighbours = (
-        has_below.astype(jnp.int32) + has_above.astype(jnp.int32)
-        + has_low.astype(jnp.int32) + has_high.astype(jnp.int32)
-    )
-    far = [(LAST, by, LAST + 1) for by in UP_BY] + [(LAST + 1, by, LAST) for by in DOWN_BY]
-    for start, by, end in far:
-        signal(p == by, barrier, {"prop": start})
-        signal(p == end, barrier, {"prop": by})
-        neighbours += (p == start).astype(jnp.int32) + (p == by).astype(jnp.int32)
     pl.semaphore_wait(barrier, neighbours)
+    for start, end, (first, *others) in sides:
+        for one in (start, *others):
+            signal(p == first, far_sem, {"prop": one})
 
     def lanes(c):
         return slice(c * chunk, (c + 1) * chunk)
@@ -212,7 +218,7 @@
         end = LAST + 1 if is_up else LAST
         return remote(passing.at[sweep, i], dst, pass_send.at[sweep, i], recv, {"prop": end})
 
-    def start_sweep(sweep):
+    def start_pass(sweep):
         for at, c, way, i in RELAYED:
             if at == sweep:
                 for is_up, start, by in ((True, LAST, UP_BY[way - 1]), (False, LAST + 1, DOWN_BY[way - 1])):
@@ -221,16 +227,28 @@
                     def _():
                         to_pass(sweep, c, i, is_up, by).start()
 
+    def start_near(sweep):
         for c in range(CHUNKS):
-            straight = WAYS[sweep][c] == 0
-
-            @pl.when(has_below if straight else has_below & (p != LAST + 1))
+
+            @pl.when(near_below)
             def _():
                 down(sweep, c).start()
 
-            @pl.when(has_above if straight else has_above & (p != LAST))
+            @pl.when(near_above)
             def _():
                 up(sweep, c).start()
+
+    def start_far(sweep):
+        for c in range(CHUNKS):
+            if WAYS[sweep][c] == 0:
+
+                @pl.when(p == LAST + 1)
+                def _():
+                    down(sweep, c).start()
+
+                @pl.when(p == LAST)
+                def _():
+                    up(sweep, c).start()
 
     def pass_all(sweep):
         for at, c, way, i in RELAYED:
@@ -242,9 +260,10 @@
                         to_pass(sweep, c, i, is_up, by).wait_recv()
                         pass_on(sweep, c, i, is_up).start()
 
-    start_sweep(0)
-
-    @pl.when(has_below)
+    start_pass(0)
+    start_near(0)
+
+    @pl.when(near_below)
     def _():
         eps_copy.start()
 
@@ -327,6 +346,20 @@
         tab[1, :, part] = jnp.broadcast_to(dense[PROFILES + i : PROFILES + i + 1, :] * inverse, (8, LANES))
         tab[2, :, part] = a * inverse
     loads[1].wait()
+
+    told = [one for start, end, (first, *others) in sides for one in (start, *others)]
+
+    @pl.when(functools.reduce(jnp.logical_or, [p == one for one in told]))
+    def _():
+        pl.semaphore_wait(far_sem, 1)
+
+    start_far(0)
+
+    @pl.when(p == LAST + 1)
+    def _():
+        eps_copy.start()
+
+    pass_all(0)
     wait_edges(0)
 
     def to_first(k, c, here, value):
@@ -338,7 +371,10 @@
             y[c, k, :, pl.ds(pl.multiple_of(here.start + LANES, LANES), here.size)] = value
 
     partial_sweep(x, rhs, low_in.at[0], high_in.at[0], tab, a, to_first, size)
-    start_sweep(1)
+    start_pass(1)
+    start_near(1)
+    start_far(1)
+    pass_all(1)
 
     for c in range(CHUNKS):
 
@@ -361,8 +397,6 @@
             y[1 - i, 4, :, wide] = q_own[1 - i, 1, :, part] - s * a * e_next[i, 0, :, part]
 
     send_edges(1, y)
-    pass_all(0)
-    pass_all(1)
 
     @pl.when(has_above)
     def _():
@@ -472,7 +506,7 @@
             pltpu.VMEM((1, listed), jnp.int32), pltpu.VMEM((1, listed), jnp.int32),
             pltpu.VMEM((3, 8, size), f32),
             *[pltpu.VMEM((2, 8, size), f32)] * 4,
-            pltpu.VMEM((2, SLOTS, 2, 2, 8, size // CHUNKS), f32), dma((2, SLOTS)), dma((2, SLOTS)),
+            pltpu.SemaphoreType.REGULAR, pltpu.VMEM((2, SLOTS, 2, 2, 8, size // CHUNKS), f32), dma((2, SLOTS)), dma((2, SLOTS)),
             dma((5,)), dma((CHUNKS + 1, 2)), dma((2,)), dma((2, 2)), dma((2, 2)),
             *[dma((2, CHUNKS))] * 4,
         ],

time: 32.8 us -> 28.1 us (0.86)
  Pallas kernels: 29.9 us -> 25.3 us
    pallas_call x1, Pallas kernels: 29.9 us -> 25.3 us  [local(): pl.pallas_call(kernel, out_shape=jax.ShapeDtypeStruct(whole, f32), in_spe...]
where the time goes in v2:
time: 28.1 us; the launch traced here: 28 us
  Pallas kernels  25.3 us (90%)
  local copies, waits for them, and re-layouts  2.06 us (7%)
  between operations  0.66 us (2%)
    pallas_call x1, Pallas kernels, local(): pl.pallas_call(kernel, out_shape=jax.ShapeDtypeStruct(whole, f32), in_spe...  25.3 us
    unnamed x1, local copies, waits for them, and re-layouts  2.06 us

profile of v2, /device:TPU:31, one launch (start us, length us, event | category | flops | bytes accessed | tf_op | source)
XLA Modules:
  0.0 28.0 jit_solution(12553722152992852009)
XLA Ops:
  0.7 25.3 %sweeps.1 = f32[2,6,8,2048]{3,2,1,0:T(8,128)} custom-call(f32[2,6,8,2048]{3,2,1,0:T(8,128)} %rhs_hbm.1, f32[2,6,8,2048]{3,2,1,0:T(8,128)} %field_hbm.1, f32[1,2048]{1,0:T(1,128)} %bitcast.1, s32[1,640]{1,0:T(1,128)} %cells_hbm.1, s32[1,640]{1,0:T(1,128)} %profile_hbm.1, s32[1]{0:T(128)S(6)} %copy.10.count, f32[16]{0:T(128)} %amp.1, f32[16]{0:T(128)} %phase.1), custom_call_target="tpu_custom_call" | custom-call | tf_op jit(solution)/shard_map/sweeps/pallas_call | solution.py:497
  25.9 2.1 %copy.11 = f32[2,6,8,2048]{3,2,1,0:T(8,128)} copy(f32[2,6,8,2048]{3,2,1,0:T(8,128)} %sweeps.1) | data formatting | bytes 1572864

commit v3 on v2

--- a/solution.py
+++ b/solution.py
@@ -18,15 +18,17 @@
 BLOCK = 512
 CHUNKS = 8
 LAST = 15
-UP_BY, DOWN_BY = (0, 3, 12), (31, 28, 19)
-WAYS = ((1, 2, 3, 0, 1, 2, 3, 0), (1, 2, 3, 0, 1, 2, 0, 0))
-SLOTS = 2
+UP_WAYS = ((0, 12, 3, None, 0, 12, 3, None), (0, 12, 3, None, 0, 12, None, None))
+DOWN_WAYS = ((19, 28, 24, None, 19, 28, 24, None), (19, 28, 24, None, 19, 28, None, None))
+UP_FIRST, DOWN_FIRST = (0, 19)
 RELAYED = [
-    (sweep, c, way, WAYS[sweep][:c].count(way))
+    (sweep, c, is_up, by, ways[sweep][:c].count(by))
+    for is_up, ways in ((True, UP_WAYS), (False, DOWN_WAYS))
     for sweep in range(2)
-    for c, way in enumerate(WAYS[sweep])
-    if way
+    for c, by in enumerate(ways[sweep])
+    if by is not None
 ]
+SLOTS = 1 + max(i for *_, i in RELAYED)
 
 
 def remote(src, dst, send, recv, device):
@@ -77,7 +79,7 @@
     )
 
 
-def partial_sweep(fields, rhs, low_edge, high_edge, tab, a, out, cells):
+def partial_sweep(fields, rhs, low_edge, high_edge, tab, a, out, cells, electric, magnetic):
     width = min(BLOCK, cells)
     wide = width + LANES
     lane = lax.broadcasted_iota(jnp.int32, (8, width), 1)
@@ -104,15 +106,18 @@
             dx = own - jnp.where(not_first, pltpu.roll(v, 1, 1)[:, LANES:], 0.0)
             return own, dy, dx
 
-        cos_t, sin_t, ae = (tab[i, :, here] for i in range(3))
+        if electric:
+            cos_t, sin_t, ae = (tab[i, :, here] for i in range(3))
         couple = []
-        for k in range(3):
+        for k in range(3 if electric else 0):
             low, high = [], []
             for c in range(2):
                 v = fields[c, k, :, mid]
                 i = c * 3 + k
-                low.append(jnp.where(row == 0, low_edge[i : i + 1, here], pltpu.roll(v, 1, 0)))
-                high.append(jnp.where(row == 7, high_edge[i : i + 1, here], pltpu.roll(v, 7, 0)))
+                first = 0.0 if low_edge is None else low_edge[i : i + 1, here]
+                last = 0.0 if high_edge is None else high_edge[i : i + 1, here]
+                low.append(jnp.where(row == 0, first, pltpu.roll(v, 1, 0)))
+                high.append(jnp.where(row == 7, last, pltpu.roll(v, 7, 0)))
             couple.append(
                 (
                     cos_t * (low[0] + high[0]) + sin_t * (high[1] - low[1]),
@@ -121,20 +126,41 @@
             )
         for c in range(2):
             s = 1.0 if c == 1 else -1.0
-            ex, ex_y, _ = ahead(c, 0)
-            ey, _, ey_x = ahead(c, 1)
-            _, ez_y, ez_x = ahead(c, 2)
-            sa = s * a
-            out(3, 1 - c, here, sa * (rhs[c, 3, :, here] - ez_y - ey))
-            out(4, 1 - c, here, sa * (rhs[c, 4, :, here] + ex + ez_x))
-            out(5, 1 - c, here, sa * (rhs[c, 5, :, here] - ey_x + ex_y))
-            hx, hx_y, _ = behind(c, 3)
-            hy, _, hy_x = behind(c, 4)
-            _, hz_y, hz_x = behind(c, 5)
-            sae = s * ae
-            out(0, 1 - c, here, sae * (rhs[c, 0, :, here] + hz_y - hy) - couple[0][1 - c])
-            out(1, 1 - c, here, sae * (rhs[c, 1, :, here] + hx - hz_x) - couple[1][1 - c])
-            out(2, 1 - c, here, sae * (rhs[c, 2, :, here] + hy_x - hx_y) - couple[2][1 - c])
+            if magnetic:
+                ex, ex_y, _ = ahead(c, 0)
+                ey, _, ey_x = ahead(c, 1)
+                _, ez_y, ez_x = ahead(c, 2)
+                sa = s * a
+                out(3, 1 - c, here, sa * (rhs[c, 3, :, here] - ez_y - ey))
+                out(4, 1 - c, here, sa * (rhs[c, 4, :, here] + ex + ez_x))
+                out(5, 1 - c, here, sa * (rhs[c, 5, :, here] - ey_x + ex_y))
+            if electric:
+                hx, hx_y, _ = behind(c, 3)
+                hy, _, hy_x = behind(c, 4)
+                _, hz_y, hz_x = behind(c, 5)
+                sae = s * ae
+                out(0, 1 - c, here, sae * (rhs[c, 0, :, here] + hz_y - hy) - couple[0][1 - c])
+                out(1, 1 - c, here, sae * (rhs[c, 1, :, here] + hx - hz_x) - couple[1][1 - c])
+                out(2, 1 - c, here, sae * (rhs[c, 2, :, here] + hy_x - hx_y) - couple[2][1 - c])
+        return carry
+
+    lax.fori_loop(0, cells // width, body, 0)
+
+
+def add_edges(low_edge, high_edge, tab, res, cells):
+    width = min(BLOCK, cells)
+    row = lax.broadcasted_iota(jnp.int32, (8, width), 0)
+
+    def body(step, carry):
+        here = pl.ds(pl.multiple_of(step * width, LANES), width)
+        cos_t, sin_t = tab[0, :, here], tab[1, :, here]
+        for k in range(3):
+            low_re, low_im, high_re, high_im = (
+                jnp.where(row == at, edge[i : i + 1, here], 0.0)
+                for at, edge, i in ((0, low_edge, k), (0, low_edge, 3 + k), (7, high_edge, k), (7, high_edge, 3 + k))
+            )
+            res[0, k, :, here] -= cos_t * (low_re + high_re) + sin_t * (high_im - low_im)
+            res[1, k, :, here] -= cos_t * (low_im + high_im) + sin_t * (low_re - high_re)
         return carry
 
     lax.fori_loop(0, cells // width, body, 0)
@@ -155,7 +181,10 @@
     has_low, has_high = h > 0, h < nh - 1
 
     near_above, near_below = has_above & (p != LAST), has_below & (p != LAST + 1)
-    sides = [(LAST, LAST + 1, UP_BY), (LAST + 1, LAST, DOWN_BY)]
+    sides = [
+        (LAST, LAST + 1, [UP_FIRST] + sorted({by for *_, is_up, by, _ in RELAYED if is_up} - {UP_FIRST})),
+        (LAST + 1, LAST, [DOWN_FIRST] + sorted({by for *_, is_up, by, _ in RELAYED if not is_up} - {DOWN_FIRST})),
+    ]
     barrier = pltpu.get_barrier_semaphore()
     signal(near_below, barrier, below)
     signal(near_above, barrier, above)
@@ -183,6 +212,57 @@
     for load in loads:
         load.start()
 
+    def pack_edges(sweep, fields):
+        for c in range(2):
+            for k in range(3):
+                i = c * 3 + k
+                low_out[sweep, i : i + 1, :] = fields[c, k, 0:1, interior]
+                high_out[sweep, i : i + 1, :] = fields[c, k, 7:8, interior]
+
+    for sweep in range(2):
+        low_out[sweep, 6:8, :] = jnp.zeros((2, size), jnp.float32)
+        high_out[sweep, 6:8, :] = jnp.zeros((2, size), jnp.float32)
+    loads[0].wait()
+    pack_edges(0, x)
+
+    @pl.when(jnp.logical_not(has_low))
+    def _():
+        low_in[...] = jnp.zeros_like(low_in)
+
+    @pl.when(jnp.logical_not(has_high))
+    def _():
+        high_in[...] = jnp.zeros_like(high_in)
+
+    @pl.when(jnp.logical_not(has_below))
+    def _():
+        h_prev[...] = jnp.zeros_like(h_prev)
+        q_prev[...] = jnp.zeros_like(q_prev)
+
+    @pl.when(jnp.logical_not(has_above))
+    def _():
+        e_next[...] = jnp.zeros_like(e_next)
+        p_next[...] = jnp.zeros_like(p_next)
+        eps_next[...] = jnp.ones_like(eps_next)
+
+    pad = jnp.zeros((2, 3, 8, LANES), jnp.float32)
+    for fields in (x, y):
+        fields[:, 0:3, :, LANES + size :] = pad
+        fields[:, 3:6, :, :LANES] = pad
+
+    harmonic = h * 8 + lax.broadcasted_iota(jnp.int32, (8, 1), 0)
+    omega = BASE_FREQUENCY + MOD_FREQUENCY * (harmonic - HARMONICS // 2).astype(jnp.float32)
+    a = 1.0 / omega
+    loads[1].wait()
+
+    def to_first(k, c, here, value):
+        if k in (0, 1):
+            p_own[c, k, :, here] = value
+        elif k in (3, 4):
+            q_own[c, k - 3, :, here] = value
+        else:
+            y[c, k, :, pl.ds(pl.multiple_of(here.start + LANES, LANES), here.size)] = value
+
+    partial_sweep(x, rhs, None, None, tab, a, to_first, size, False, True)
     pl.semaphore_wait(barrier, neighbours)
     for start, end, (first, *others) in sides:
         for one in (start, *others):
@@ -218,54 +298,42 @@
         end = LAST + 1 if is_up else LAST
         return remote(passing.at[sweep, i], dst, pass_send.at[sweep, i], recv, {"prop": end})
 
-    def start_pass(sweep):
-        for at, c, way, i in RELAYED:
-            if at == sweep:
-                for is_up, start, by in ((True, LAST, UP_BY[way - 1]), (False, LAST + 1, DOWN_BY[way - 1])):
-
-                    @pl.when(p == start)
-                    def _():
-                        to_pass(sweep, c, i, is_up, by).start()
-
-    def start_near(sweep):
+    def start_pass(sweep, upward):
+        for at, c, is_up, by, i in RELAYED:
+            if at == sweep and is_up == upward:
+
+                @pl.when(p == (LAST if is_up else LAST + 1))
+                def _():
+                    to_pass(sweep, c, i, is_up, by).start()
+
+    def start_near(sweep, upward):
         for c in range(CHUNKS):
 
-            @pl.when(near_below)
+            @pl.when(near_above if upward else near_below)
             def _():
-                down(sweep, c).start()
-
-            @pl.when(near_above)
-            def _():
-                up(sweep, c).start()
-
-    def start_far(sweep):
+                (up if upward else down)(sweep, c).start()
+
+    def start_far(sweep, upward):
         for c in range(CHUNKS):
-            if WAYS[sweep][c] == 0:
-
-                @pl.when(p == LAST + 1)
+            if (UP_WAYS if upward else DOWN_WAYS)[sweep][c] is None:
+
+                @pl.when(p == (LAST if upward else LAST + 1))
                 def _():
-                    down(sweep, c).start()
-
-                @pl.when(p == LAST)
+                    (up if upward else down)(sweep, c).start()
+
+    def pass_all(sweep, by_first):
+        for at, c, is_up, by, i in RELAYED:
+            if at == sweep and by_first == (by in (UP_FIRST, DOWN_FIRST)):
+
+                @pl.when(p == by)
                 def _():
-                    up(sweep, c).start()
-
-    def pass_all(sweep):
-        for at, c, way, i in RELAYED:
-            if at == sweep:
-                for is_up, by in ((True, UP_BY[way - 1]), (False, DOWN_BY[way - 1])):
-
-                    @pl.when(p == by)
-                    def _():
-                        to_pass(sweep, c, i, is_up, by).wait_recv()
-                        pass_on(sweep, c, i, is_up).start()
-
-    start_pass(0)
-    start_near(0)
-
-    @pl.when(near_below)
-    def _():
-        eps_copy.start()
+                    to_pass(sweep, c, i, is_up, by).wait_recv()
+                    pass_on(sweep, c, i, is_up).start()
+
+    def wait_far(slabs):
+        @pl.when(functools.reduce(jnp.logical_or, [p == one for one in slabs]))
+        def _():
+            pl.semaphore_wait(far_sem, 1)
 
     def to_low(sweep):
         return remote(
@@ -279,13 +347,7 @@
             {"harm": h + 1},
         )
 
-    def send_edges(sweep, fields):
-        for c in range(2):
-            for k in range(3):
-                i = c * 3 + k
-                low_out[sweep, i : i + 1, :] = fields[c, k, 0:1, interior]
-                high_out[sweep, i : i + 1, :] = fields[c, k, 7:8, interior]
-
+    def send_edges(sweep):
         @pl.when(has_low)
         def _():
             to_low(sweep).start()
@@ -303,39 +365,18 @@
         def _():
             to_high(sweep).wait_recv()
 
-    for sweep in range(2):
-        low_out[sweep, 6:8, :] = jnp.zeros((2, size), jnp.float32)
-        high_out[sweep, 6:8, :] = jnp.zeros((2, size), jnp.float32)
-    loads[0].wait()
-    send_edges(0, x)
-
-    @pl.when(jnp.logical_not(has_low))
-    def _():
-        low_in[...] = jnp.zeros_like(low_in)
-
-    @pl.when(jnp.logical_not(has_high))
-    def _():
-        high_in[...] = jnp.zeros_like(high_in)
-
-    @pl.when(jnp.logical_not(has_below))
-    def _():
-        h_prev[...] = jnp.zeros_like(h_prev)
-        q_prev[...] = jnp.zeros_like(q_prev)
-
-    @pl.when(jnp.logical_not(has_above))
-    def _():
-        e_next[...] = jnp.zeros_like(e_next)
-        p_next[...] = jnp.zeros_like(p_next)
-        eps_next[...] = jnp.ones_like(eps_next)
-
-    pad = jnp.zeros((2, 3, 8, LANES), jnp.float32)
-    for fields in (x, y):
-        fields[:, 0:3, :, LANES + size :] = pad
-        fields[:, 3:6, :, :LANES] = pad
-
-    harmonic = h * 8 + lax.broadcasted_iota(jnp.int32, (8, 1), 0)
-    omega = BASE_FREQUENCY + MOD_FREQUENCY * (harmonic - HARMONICS // 2).astype(jnp.float32)
-    a = 1.0 / omega
+    send_edges(0)
+    for upward in (True, False):
+        start_pass(0, upward)
+    start_pass(1, True)
+    for upward in (True, False):
+        start_near(0, upward)
+    start_near(1, True)
+
+    @pl.when(near_below)
+    def _():
+        eps_copy.start()
+
     for load in loads[2:]:
         load.wait()
     dense = mod_tables(p.astype(jnp.float32), cells[...], profile[...], count, amp, phase)
@@ -345,36 +386,27 @@
         tab[0, :, part] = jnp.broadcast_to(dense[i : i + 1, :] * inverse, (8, LANES))
         tab[1, :, part] = jnp.broadcast_to(dense[PROFILES + i : PROFILES + i + 1, :] * inverse, (8, LANES))
         tab[2, :, part] = a * inverse
-    loads[1].wait()
-
-    told = [one for start, end, (first, *others) in sides for one in (start, *others)]
-
-    @pl.when(functools.reduce(jnp.logical_or, [p == one for one in told]))
-    def _():
-        pl.semaphore_wait(far_sem, 1)
-
-    start_far(0)
+
+    wait_far((LAST, LAST + 1))
+    for upward in (True, False):
+        start_far(0, upward)
+    start_far(1, True)
 
     @pl.when(p == LAST + 1)
     def _():
         eps_copy.start()
 
-    pass_all(0)
+    pass_all(0, True)
     wait_edges(0)
 
-    def to_first(k, c, here, value):
-        if k in (0, 1):
-            p_own[c, k, :, here] = value
-        elif k in (3, 4):
-            q_own[c, k - 3, :, here] = value
-        else:
-            y[c, k, :, pl.ds(pl.multiple_of(here.start + LANES, LANES), here.size)] = value
-
-    partial_sweep(x, rhs, low_in.at[0], high_in.at[0], tab, a, to_first, size)
-    start_pass(1)
-    start_near(1)
-    start_far(1)
-    pass_all(1)
+    partial_sweep(x, rhs, low_in.at[0], high_in.at[0], tab, a, to_first, size, True, False)
+    start_pass(1, False)
+    start_near(1, False)
+    wait_far([one for _, _, (_, *others) in sides for one in others])
+    start_far(1, False)
+    pass_all(0, False)
+    pass_all(1, True)
+    pass_all(1, False)
 
     for c in range(CHUNKS):
 
@@ -396,7 +428,8 @@
             y[1 - i, 3, :, wide] = q_own[1 - i, 0, :, part] + s * a * e_next[i, 1, :, part]
             y[1 - i, 4, :, wide] = q_own[1 - i, 1, :, part] - s * a * e_next[i, 0, :, part]
 
-    send_edges(1, y)
+    pack_edges(1, y)
+    send_edges(1)
 
     @pl.when(has_above)
     def _():
@@ -404,12 +437,13 @@
 
     above_factor = has_above.astype(jnp.float32)
     below_factor = has_below.astype(jnp.float32)
-    wait_edges(1)
 
     def to_second(k, c, here, value):
         res[c, k, :, here] = value
 
-    partial_sweep(y, rhs, low_in.at[1], high_in.at[1], tab, a, to_second, size)
+    partial_sweep(y, rhs, None, None, tab, a, to_second, size, True, True)
+    wait_edges(1)
+    add_edges(low_in.at[1], high_in.at[1], tab, res, size)
     outs = [
         pltpu.make_async_copy(res.at[:, k], out_hbm.at[:, k], out_sem.at[0, i])
         for i, k in enumerate((2, 5))
@@ -474,12 +508,11 @@
             def _():
                 up(sweep, c).wait_send()
 
-    for sweep, c, way, i in RELAYED:
-        for is_up, by in ((True, UP_BY[way - 1]), (False, DOWN_BY[way - 1])):
-
-            @pl.when(p == by)
-            def _():
-                pass_on(sweep, c, i, is_up).wait_send()
+    for sweep, c, is_up, by, i in RELAYED:
+
+        @pl.when(p == by)
+        def _():
+            pass_on(sweep, c, i, is_up).wait_send()
 
     for copy in outs:
         copy.wait()

time: 28.1 us -> 26.6 us (0.947); the launches traced: 28 us -> 26.2 us
  Pallas kernels: 25.3 us -> 23.4 us
    pallas_call x1, Pallas kernels: 25.3 us -> 23.4 us  [local(): pl.pallas_call(kernel, out_shape=jax.ShapeDtypeStruct(whole, f32), in_spe...]
where the time goes in v3:
time: 26.6 us; the launch traced here: 26.2 us
  Pallas kernels  23.4 us (88%)
  local copies, waits for them, and re-layouts  2.06 us (8%)
  between operations  0.66 us (2%)
    pallas_call x1, Pallas kernels, local(): pl.pallas_call(kernel, out_shape=jax.ShapeDtypeStruct(whole, f32), in_spe...  23.4 us
    unnamed x1, local copies, waits for them, and re-layouts  2.06 us

profile of v3, /device:TPU:31, one launch (start us, length us, event | category | flops | bytes accessed | tf_op | source)
XLA Modules:
  0.0 26.2 jit_solution(18142087716515121201)
XLA Ops:
  0.7 23.4 %sweeps.1 = f32[2,6,8,2048]{3,2,1,0:T(8,128)} custom-call(f32[2,6,8,2048]{3,2,1,0:T(8,128)} %rhs_hbm.1, f32[2,6,8,2048]{3,2,1,0:T(8,128)} %field_hbm.1, f32[1,2048]{1,0:T(1,128)} %bitcast.1, s32[1,640]{1,0:T(1,128)} %cells_hbm.1, s32[1,640]{1,0:T(1,128)} %profile_hbm.1, s32[1]{0:T(128)S(6)} %copy.10.count, f32[16]{0:T(128)} %amp.1, f32[16]{0:T(128)} %phase.1), custom_call_target="tpu_custom_call" | custom-call | tf_op jit(solution)/shard_map/sweeps/pallas_call | solution.py:530
  24.1 2.1 %copy.11 = f32[2,6,8,2048]{3,2,1,0:T(8,128)} copy(f32[2,6,8,2048]{3,2,1,0:T(8,128)} %sweeps.1) | data formatting | bytes 1572864

commit v4 on v3

--- a/solution.py
+++ b/solution.py
@@ -18,7 +18,7 @@
 BLOCK = 512
 CHUNKS = 8
 LAST = 15
-UP_WAYS = ((0, 12, 3, None, 0, 12, 3, None), (0, 12, 3, None, 0, 12, None, None))
+UP_WAYS = ((0, 12, 3, None, 0, 12, 3, 0), (12, 0, None, 3, 12, None, None, None))
 DOWN_WAYS = ((19, 28, 24, None, 19, 28, 24, None), (19, 28, 24, None, 19, 28, None, None))
 UP_FIRST, DOWN_FIRST = (0, 19)
 RELAYED = [
@@ -147,30 +147,23 @@
     lax.fori_loop(0, cells // width, body, 0)
 
 
-def add_edges(low_edge, high_edge, tab, res, cells):
-    width = min(BLOCK, cells)
-    row = lax.broadcasted_iota(jnp.int32, (8, width), 0)
-
-    def body(step, carry):
-        here = pl.ds(pl.multiple_of(step * width, LANES), width)
-        cos_t, sin_t = tab[0, :, here], tab[1, :, here]
-        for k in range(3):
-            low_re, low_im, high_re, high_im = (
-                jnp.where(row == at, edge[i : i + 1, here], 0.0)
-                for at, edge, i in ((0, low_edge, k), (0, low_edge, 3 + k), (7, high_edge, k), (7, high_edge, 3 + k))
-            )
-            res[0, k, :, here] -= cos_t * (low_re + high_re) + sin_t * (high_im - low_im)
-            res[1, k, :, here] -= cos_t * (low_im + high_im) + sin_t * (low_re - high_re)
-        return carry
-
-    lax.fori_loop(0, cells // width, body, 0)
+def add_edges(low_edge, high_edge, tab, res, here):
+    row = lax.broadcasted_iota(jnp.int32, (8, here.stop - here.start), 0)
+    cos_t, sin_t = tab[0, :, here], tab[1, :, here]
+    for k in range(3):
+        low_re, low_im, high_re, high_im = (
+            jnp.where(row == at, edge[i : i + 1, here], 0.0)
+            for at, edge, i in ((0, low_edge, k), (0, low_edge, 3 + k), (7, high_edge, k), (7, high_edge, 3 + k))
+        )
+        res[0, k, :, here] -= cos_t * (low_re + high_re) + sin_t * (high_im - low_im)
+        res[1, k, :, here] -= cos_t * (low_im + high_im) + sin_t * (low_re - high_re)
 
 
 def kernel(
     rhs_hbm, field_hbm, eps_hbm, cells_hbm, profile_hbm, count, amp, phase, out_hbm,
     x, y, rhs, res, p_own, q_own, e_next, h_prev, p_next, q_prev, eps, eps_next, cells, profile,
     tab, low_out, high_out, low_in, high_in,
-    far_sem, passing, pass_recv, pass_send, local_sem, out_sem, eps_sem, edge_send, edge_recv, down_send, down_recv, up_send, up_recv,
+    last_sem, far_sem, passing, pass_recv, pass_send, local_sem, out_sem, eps_sem, edge_send, edge_recv, down_send, down_recv, up_send, up_recv,
 ):
     h, p = lax.axis_index("harm"), lax.axis_index("prop")
     nh, np_ = lax.axis_size("harm"), lax.axis_size("prop")
@@ -442,11 +435,9 @@
         res[c, k, :, here] = value
 
     partial_sweep(y, rhs, None, None, tab, a, to_second, size, True, True)
-    wait_edges(1)
-    add_edges(low_in.at[1], high_in.at[1], tab, res, size)
     outs = [
         pltpu.make_async_copy(res.at[:, k], out_hbm.at[:, k], out_sem.at[0, i])
-        for i, k in enumerate((2, 5))
+        for i, k in enumerate((5,))
     ]
     for copy in outs:
         copy.start()
@@ -477,12 +468,23 @@
             res[j, 1, :, part] -= s * ae * hx
             res[j, 3, :, part] += s * a * ey
             res[j, 4, :, part] -= s * a * ex
-        for i, k in enumerate((0, 3)):
+        for i, k in enumerate((3,)):
             copy = pltpu.make_async_copy(
                 res.at[:, k : k + 2, :, part], out_hbm.at[:, k : k + 2, :, part], out_sem.at[c + 1, i]
             )
             copy.start()
             outs.append(copy)
+
+    wait_edges(1)
+    block = min(BLOCK, size)
+    for i in range(size // block):
+        part = slice(i * block, (i + 1) * block)
+        add_edges(low_in.at[1], high_in.at[1], tab, res, part)
+        copy = pltpu.make_async_copy(
+            res.at[:, 0:3, :, part], out_hbm.at[:, 0:3, :, part], last_sem.at[i]
+        )
+        copy.start()
+        outs.append(copy)
 
     @pl.when(has_below)
     def _():
@@ -539,7 +541,7 @@
             pltpu.VMEM((1, listed), jnp.int32), pltpu.VMEM((1, listed), jnp.int32),
             pltpu.VMEM((3, 8, size), f32),
             *[pltpu.VMEM((2, 8, size), f32)] * 4,
-            pltpu.SemaphoreType.REGULAR, pltpu.VMEM((2, SLOTS, 2, 2, 8, size // CHUNKS), f32), dma((2, SLOTS)), dma((2, SLOTS)),
+            dma((max(1, size // BLOCK),)), pltpu.SemaphoreType.REGULAR, pltpu.VMEM((2, SLOTS, 2, 2, 8, size // CHUNKS), f32), dma((2, SLOTS)), dma((2, SLOTS)),
             dma((5,)), dma((CHUNKS + 1, 2)), dma((2,)), dma((2, 2)), dma((2, 2)),
             *[dma((2, CHUNKS))] * 4,
         ],

time: 26.6 us -> 26.3 us (0.989)
  no operation moved by 1% of the time
where the time goes in v4:
time: 26.3 us; the launch traced here: 26.1 us
  Pallas kernels  23.4 us (89%)
  local copies, waits for them, and re-layouts  2.06 us (8%)
  between operations  0.66 us (3%)
    pallas_call x1, Pallas kernels, local(): pl.pallas_call(kernel, out_shape=jax.ShapeDtypeStruct(whole, f32), in_spe...  23.4 us
    unnamed x1, local copies, waits for them, and re-layouts  2.06 us

profile of v4, /device:TPU:31, one launch (start us, length us, event | category | flops | bytes accessed | tf_op | source)
XLA Modules:
  0.0 26.1 jit_solution(11741468986431262307)
XLA Ops:
  0.7 23.4 %sweeps.1 = f32[2,6,8,2048]{3,2,1,0:T(8,128)} custom-call(f32[2,6,8,2048]{3,2,1,0:T(8,128)} %rhs_hbm.1, f32[2,6,8,2048]{3,2,1,0:T(8,128)} %field_hbm.1, f32[1,2048]{1,0:T(1,128)} %bitcast.1, s32[1,640]{1,0:T(1,128)} %cells_hbm.1, s32[1,640]{1,0:T(1,128)} %profile_hbm.1, s32[1]{0:T(128)S(6)} %copy.10.count, f32[16]{0:T(128)} %amp.1, f32[16]{0:T(128)} %phase.1), custom_call_target="tpu_custom_call" | custom-call | tf_op jit(solution)/shard_map/sweeps/pallas_call | solution.py:532
  24.0 2.1 %copy.11 = f32[2,6,8,2048]{3,2,1,0:T(8,128)} copy(f32[2,6,8,2048]{3,2,1,0:T(8,128)} %sweeps.1) | data formatting | bytes 1572864

commit v5 on v4

--- a/solution.py
+++ b/solution.py
@@ -179,10 +179,6 @@
         (LAST + 1, LAST, [DOWN_FIRST] + sorted({by for *_, is_up, by, _ in RELAYED if not is_up} - {DOWN_FIRST})),
     ]
     barrier = pltpu.get_barrier_semaphore()
-    signal(near_below, barrier, below)
-    signal(near_above, barrier, above)
-    signal(has_low, barrier, {"harm": h - 1})
-    signal(has_high, barrier, {"harm": h + 1})
     neighbours = sum(
         condition.astype(jnp.int32) for condition in (near_below, near_above, has_low, has_high)
     )
@@ -193,6 +189,11 @@
         for source, target in greetings:
             signal(p == source, barrier, {"prop": target})
             neighbours += (p == target).astype(jnp.int32)
+
+    signal(near_below, barrier, below)
+    signal(near_above, barrier, above)
+    signal(has_low, barrier, {"harm": h - 1})
+    signal(has_high, barrier, {"harm": h + 1})
 
     interior = slice(LANES, LANES + size)
     loads = [

time: 26.3 us -> 26.3 us (level)
  no operation moved by 1% of the time
where the time goes in v5:
time: 26.3 us; the launch traced here: 25.9 us
  Pallas kernels  23.2 us (88%)
  local copies, waits for them, and re-layouts  2.06 us (8%)
  between operations  0.66 us (3%)
    pallas_call x1, Pallas kernels, local(): pl.pallas_call(kernel, out_shape=jax.ShapeDtypeStruct(whole, f32), in_spe...  23.2 us
    unnamed x1, local copies, waits for them, and re-layouts  2.06 us

profile of v5, /device:TPU:31, one launch (start us, length us, event | category | flops | bytes accessed | tf_op | source)
XLA Modules:
  0.0 25.9 jit_solution(12031912554528826065)
XLA Ops:
  0.7 23.2 %sweeps.1 = f32[2,6,8,2048]{3,2,1,0:T(8,128)} custom-call(f32[2,6,8,2048]{3,2,1,0:T(8,128)} %rhs_hbm.1, f32[2,6,8,2048]{3,2,1,0:T(8,128)} %field_hbm.1, f32[1,2048]{1,0:T(1,128)} %bitcast.1, s32[1,640]{1,0:T(1,128)} %cells_hbm.1, s32[1,640]{1,0:T(1,128)} %profile_hbm.1, s32[1]{0:T(128)S(6)} %copy.10.count, f32[16]{0:T(128)} %amp.1, f32[16]{0:T(128)} %phase.1), custom_call_target="tpu_custom_call" | custom-call | tf_op jit(solution)/shard_map/sweeps/pallas_call | solution.py:533
  23.9 2.1 %copy.11 = f32[2,6,8,2048]{3,2,1,0:T(8,128)} copy(f32[2,6,8,2048]{3,2,1,0:T(8,128)} %sweeps.1) | data formatting | bytes 1572864

commit v6 on v5

--- a/solution.py
+++ b/solution.py
@@ -147,16 +147,18 @@
     lax.fori_loop(0, cells // width, body, 0)
 
 
-def add_edges(low_edge, high_edge, tab, res, here):
+def add_edges(low_edge, high_edge, tab, places, here):
     row = lax.broadcasted_iota(jnp.int32, (8, here.stop - here.start), 0)
     cos_t, sin_t = tab[0, :, here], tab[1, :, here]
     for k in range(3):
         low_re, low_im, high_re, high_im = (
-            jnp.where(row == at, edge[i : i + 1, here], 0.0)
-            for at, edge, i in ((0, low_edge, k), (0, low_edge, 3 + k), (7, high_edge, k), (7, high_edge, 3 + k))
+            jnp.where(row == side, edge[i : i + 1, here], 0.0)
+            for side, edge, i in ((0, low_edge, k), (0, low_edge, 3 + k), (7, high_edge, k), (7, high_edge, 3 + k))
         )
-        res[0, k, :, here] -= cos_t * (low_re + high_re) + sin_t * (high_im - low_im)
-        res[1, k, :, here] -= cos_t * (low_im + high_im) + sin_t * (low_re - high_re)
+        res, at, start = places[k]
+        there = slice(here.start + start, here.stop + start)
+        res[0, at, :, there] -= cos_t * (low_re + high_re) + sin_t * (high_im - low_im)
+        res[1, at, :, there] -= cos_t * (low_im + high_im) + sin_t * (low_re - high_re)
 
 
 def kernel(
@@ -381,6 +383,7 @@
         tab[1, :, part] = jnp.broadcast_to(dense[PROFILES + i : PROFILES + i + 1, :] * inverse, (8, LANES))
         tab[2, :, part] = a * inverse
 
+    partial_sweep(x, rhs, None, None, tab, a, to_first, size, True, False)
     wait_far((LAST, LAST + 1))
     for upward in (True, False):
         start_far(0, upward)
@@ -393,7 +396,9 @@
     pass_all(0, True)
     wait_edges(0)
 
-    partial_sweep(x, rhs, low_in.at[0], high_in.at[0], tab, a, to_first, size, True, False)
+    places = [(p_own, 0, 0), (p_own, 1, 0), (y, 2, LANES)]
+    for i in range(size // min(BLOCK, size)):
+        add_edges(low_in.at[0], high_in.at[0], tab, places, slice(i * BLOCK, (i + 1) * BLOCK))
     start_pass(1, False)
     start_near(1, False)
     wait_far([one for _, _, (_, *others) in sides for one in others])
@@ -480,7 +485,7 @@
     block = min(BLOCK, size)
     for i in range(size // block):
         part = slice(i * block, (i + 1) * block)
-        add_edges(low_in.at[1], high_in.at[1], tab, res, part)
+        add_edges(low_in.at[1], high_in.at[1], tab, [(res, k, 0) for k in range(3)], part)
         copy = pltpu.make_async_copy(
             res.at[:, 0:3, :, part], out_hbm.at[:, 0:3, :, part], last_sem.at[i]
         )

time: 26.3 us -> 26.4 us (level)
  Pallas kernels: 23.2 us -> 23.5 us
    pallas_call x1, Pallas kernels: 23.2 us -> 23.5 us  [local(): pl.pallas_call(kernel, out_shape=jax.ShapeDtypeStruct(whole, f32), in_spe...]
where the time goes in v6:
time: 26.4 us; the launch traced here: 26.3 us
  Pallas kernels  23.5 us (89%)
  local copies, waits for them, and re-layouts  2.06 us (8%)
  between operations  0.66 us (2%)
    pallas_call x1, Pallas kernels, local(): pl.pallas_call(kernel, out_shape=jax.ShapeDtypeStruct(whole, f32), in_spe...  23.5 us
    unnamed x1, local copies, waits for them, and re-layouts  2.06 us

profile of v6, /device:TPU:31, one launch (start us, length us, event | category | flops | bytes accessed | tf_op | source)
XLA Modules:
  0.0 26.3 jit_solution(7400023654472524438)
XLA Ops:
  0.7 23.5 %sweeps.1 = f32[2,6,8,2048]{3,2,1,0:T(8,128)} custom-call(f32[2,6,8,2048]{3,2,1,0:T(8,128)} %rhs_hbm.1, f32[2,6,8,2048]{3,2,1,0:T(8,128)} %field_hbm.1, f32[1,2048]{1,0:T(1,128)} %bitcast.1, s32[1,640]{1,0:T(1,128)} %cells_hbm.1, s32[1,640]{1,0:T(1,128)} %profile_hbm.1, s32[1]{0:T(128)S(6)} %copy.10.count, f32[16]{0:T(128)} %amp.1, f32[16]{0:T(128)} %phase.1), custom_call_target="tpu_custom_call" | custom-call | tf_op jit(solution)/shard_map/sweeps/pallas_call | solution.py:538
  24.2 2.1 %copy.11 = f32[2,6,8,2048]{3,2,1,0:T(8,128)} copy(f32[2,6,8,2048]{3,2,1,0:T(8,128)} %sweeps.1) | data formatting | bytes 1572864
